TPU v7x, 128 devices: a whole 4x4x4 slice. The times are simulated.
128 devices in a mesh: lev: 4 (over y), col: 32 (over x, z, core).
Axes of the slice: x: 4, y: 4, z: 4, core: 2. Of those that a mesh axis runs over, the one named last changes fastest.
Arguments:
- increment: bfloat16 [3, 128, 131072], P(None, 'lev', 'col'), may hold values from -6 to 6
- jacobian: bfloat16 [1024, 616, 384], P(('lev', 'col')), may hold values from -0.3125 to 0.3125
- departure: bfloat16 [616, 1048576], P(None, ('lev', 'col')), may hold values from -6 to 6
- predictor: float32 [8, 1048576], P(None, ('lev', 'col')), may hold values from -5 to 5
- bias_coef: float32 [616, 8], replicated, may hold values from -1.5 to 1.5
- obs_sigma: float32 [616], replicated, may hold values from 0.5 to 2
- channel_use: int32 [1024, 616], P(('lev', 'col')), may hold values 0 or 1
- send_cols: int32 [128, 128, 8], P(('lev', 'col')), may hold values from 0 to 1023
- obs_slot: int32 [1048576], P(('lev', 'col')), may hold values from 0 to 1023, as said below
Outputs:
- gradient: float32 [3, 128, 131072], P(None, 'lev', 'col')
Inputs may be any that keep to these rules, and one draw needn't show every extreme that they name: obs_slot[j] = s * 8 + k; the slots (s, p, k) named by the observations of device p are, for each s, the first few of the 8, at least 2 of them; some device p names all 8 slots of every device.
All inputs are finite; a program needn't handle non-finite values. No bound on the sum of `channel_use` on one device may be relied on, other than what follows from the above.
Results may differ from a plain program's by a relative error of at most 0.001.
Values may be sent and summed in bfloat16 or wider, within the bound.
A program may use at most 128 MiB of HBM per device.

v0:
```python
import jax
import jax.numpy as jnp
from jax import lax
from jax.sharding import PartitionSpec as P


def fetch_rows(outgoing):
    return lax.all_to_all(outgoing, ("lev", "col"), split_axis=0, concat_axis=0, tiled=True)


def return_rows(outgoing):
    return lax.all_to_all(outgoing, ("lev", "col"), split_axis=0, concat_axis=0, tiled=True)


def observe(profile, jacobian, departure, predictor, bias_coef, obs_sigma, channel_use):
    tile_count = jacobian.shape[0]
    channels = jacobian.shape[1]
    obs_count = profile.shape[0]
    profile_len = profile.shape[1]
    obs_tile = obs_count // tile_count
    tangent = jnp.einsum(
        "tcf,tof->cto",
        jacobian,
        profile.reshape(tile_count, obs_tile, profile_len),
        preferred_element_type=jnp.float32,
    )
    bias_term = jnp.dot(
        bias_coef, predictor, precision=lax.Precision.HIGHEST, preferred_element_type=jnp.float32
    )
    residual = tangent - (departure.astype(jnp.float32) - bias_term).reshape(
        channels, tile_count, obs_tile
    )
    inverse_var = 1.0 / (obs_sigma * obs_sigma)
    scaling = channel_use.astype(jnp.float32).T * inverse_var[:, None]
    forcing = (scaling[:, :, None] * residual).astype(jnp.bfloat16)
    return jnp.einsum(
        "tcf,cto->tof", jacobian, forcing, preferred_element_type=jnp.float32
    ).reshape(obs_count, profile_len)


def on_device(
    increment,
    jacobian,
    departure,
    predictor,
    bias_coef,
    obs_sigma,
    channel_use,
    send_cols,
    obs_slot,
):
    lev_size = lax.axis_size("lev")
    col_size = lax.axis_size("col")
    peer_count = lev_size * col_size
    field_count = increment.shape[0]
    capacity = send_cols.shape[2]
    columns = lax.all_to_all(increment, "lev", split_axis=2, concat_axis=1, tiled=True)
    level_count = columns.shape[1]
    column_count = columns.shape[2]
    profile_len = field_count * level_count
    column_rows = columns.reshape(profile_len, column_count).T
    slot_lists = send_cols[0]
    outgoing = column_rows[slot_lists]
    incoming = fetch_rows(outgoing).reshape(peer_count * capacity, profile_len)
    profile = incoming[obs_slot]
    adjoint = observe(profile, jacobian, departure, predictor, bias_coef, obs_sigma, channel_use)
    slot_adjoint = jax.ops.segment_sum(adjoint, obs_slot, num_segments=peer_count * capacity)
    returned = return_rows(slot_adjoint.reshape(peer_count, capacity, profile_len))
    column_adjoint = jax.ops.segment_sum(
        returned.reshape(peer_count * capacity, profile_len),
        slot_lists.reshape(-1),
        num_segments=column_count,
    )
    field_adjoint = column_adjoint.T.reshape(field_count, level_count, column_count)
    return lax.all_to_all(field_adjoint, "lev", split_axis=1, concat_axis=2, tiled=True)


def solution(mesh):
    return jax.shard_map(
        on_device,
        mesh=mesh,
        in_specs=(
            P(None, "lev", "col"),
            P(("lev", "col"), None, None),
            P(None, ("lev", "col")),
            P(None, ("lev", "col")),
            P(),
            P(),
            P(("lev", "col"), None),
            P(("lev", "col"), None, None),
            P(("lev", "col")),
        ),
        out_specs=P(None, "lev", "col"),
        check_vma=False,
    )
```

profile of v0, /device:TPU:0, one launch (start us, length us, event | category | flops | bytes accessed | tf_op | source)
XLA Modules:
  0.0 255.4 jit_solution(5134098283058532032)
XLA Ops:
  0.0 0.0 copy-start
  0.0 6.0 %copy.31 = bf16[3,32,4096]{1,0,2:T(4,128)(2,1)} copy(bf16[3,32,4096]{2,1,0:T(8,128)(2,1)} %param.9) | data formatting | bytes 1572864 | tf_op args[0]
  6.0 5.6 %reshape.103 = bf16[4,2,49152]{2,1,0:T(2,128)(2,1)} reshape(bf16[4096,3,32]{2,1,0:T(4,128)(2,1)} %bitcast.49) | data formatting | bytes 1572864
  11.6 4.5 %all-to-all-start = ((bf16[4,2,49152]{2,1,0:T(2,128)(2,1)}), bf16[4,2,49152]{2,1,0:T(2,128)(2,1)S(1)}, u32[]{:S(2)}, u32[]{:S(2)}) async-start(bf16[4,2,49152]{2,1,0:T(2,128)(2,1)} %reshape.103), calls=%async_computation | async-start | bytes 1572864 | tf_op jit(solution)/shard_map/all_to_all | solution.py:57
  16.2 0.0 copy-done.5
  16.2 0.1 copy.35
  16.3 0.1 reshape.65
  16.4 0.0 copy-done.6
  16.5 12.0 %all-to-all-done = bf16[4,2,49152]{2,1,0:T(2,128)(2,1)S(1)} async-done(((bf16[4,2,49152]{2,1,0:T(2,128)(2,1)}), bf16[4,2,49152]{2,1,0:T(2,128)(2,1)S(1)}, u32[]{:S(2)}, u32[]{:S(2)}) %all-to-all-start) | async-done | bytes 786464 | tf_op jit(solution)/shard_map/all_to_all | solution.py:57
  28.5 4.2 %reshape.104 = bf16[4096,3,32]{2,1,0:T(4,128)(2,1)} reshape(bf16[4,2,49152]{2,1,0:T(2,128)(2,1)S(1)} %all-to-all-done) | data formatting | bytes 1572864
  32.6 5.3 %copy.33 = bf16[3,4,32,1024]{3,2,1,0:T(8,128)(2,1)S(1)} copy(bf16[3,4,32,1024]{2,0,3,1:T(4,128)(2,1)} %bitcast.48) | data formatting | bytes 1572864 | tf_op jit(solution)/shard_map/all_to_all | solution.py:57
  38.0 0.4 copy.34
  38.3 0.0 copy-start.3
  38.4 5.0 %gather_fusion = bf16[1024,384]{1,0:T(8,128)(2,1)} fusion(bf16[1024,384]{1,0:T(8,128)(2,1)S(1)} %bitcast.46, s32[1024]{0:T(1024)S(1)} %broadcast_clamp_fusion), kind=kCustom, calls=%fused_computation | custom fusion | bytes 1576960 | tf_op jit(solution)/shard_map/gather | solution.py:63
  43.4 9.2 %all-to-all-start.1 = ((bf16[128,8,384]{2,1,0:T(8,128)(2,1)}), bf16[128,8,384]{2,1,0:T(8,128)(2,1)S(1)}, u32[]{:S(2)}, u32[]{:S(2)}) async-start(bf16[128,8,384]{2,1,0:T(8,128)(2,1)} %bitcast.7), calls=%async_computation.1 | async-start | bytes 1572864 | tf_op jit(solution)/shard_map/all_to_all | solution.py:8
  52.6 20.8 %convert_subtract_fusion = f32[616,8192]{1,0:T(8,128)} fusion(bf16[616,8192]{1,0:T(8,128)(2,1)} %param.11, f32[616,8]{0,1:T(8,128)S(1)} %copy-done.3, f32[8,8192]{1,0:T(8,128)S(1)} %copy-done), kind=kOutput, calls=%fused_computation.7 | convolution fusion | flops 494534656 | bytes 30559488 | tf_op jit(solution)/shard_map/dot_general | solution.py:27
  73.4 0.0 all-to-all-done.1
  73.4 33.1 %gather_fusion.1 = bf16[8192,384]{1,0:T(8,128)(2,1)} fusion(bf16[1024,384]{1,0:T(8,128)(2,1)S(1)} %bitcast.45, s32[8192]{0:T(1024)S(1)} %fusion.12), kind=kCustom, calls=%fused_computation.1 | custom fusion | bytes 12615680 | tf_op jit(solution)/shard_map/gather | solution.py:65
  106.5 24.5 %fusion.2 = f32[8,1024,384]{2,1,0:T(8,128)} fusion(bf16[8,616,384]{2,1,0:T(8,128)(2,1)} %param.10, f32[77,8,8,1024]{3,2,1,0:T(8,128)} %bitcast.47, f32[616,8]{0,1:T(8,128)S(1)} %multiply_bitcast_fusion, bf16[8,1024,384]{2,1,0:T(8,128)(2,1)} %bitcast.50), kind=kOutput, calls=%fused_computation.8 | convolution fusion | flops 7766212608 | bytes 42863872 | tf_op jit(solution)/shard_map/tcf,cto->tof/dot_general | solution.py:36
  131.0 50.4 %scatter_custom_fusion = f32[1024,384]{1,0:T(8,128)} fusion(s32[8192]{0:T(1024)S(1)} %copy-done.2, f32[8192,384]{1,0:T(8,128)} %bitcast.55, f32[]{:T(128)} %constant.4.clone.1), kind=kCustom, calls=%fused_computation.14 | custom fusion | flops 3145728 | bytes 1573376 | tf_op jit(solution)/shard_map/scatter-add | solution.py:67
  181.5 9.6 %all-to-all-start.2 = ((f32[128,8,384]{2,1,0:T(8,128)}), f32[128,8,384]{2,1,0:T(8,128)S(1)}, u32[]{:S(2)}, u32[]{:S(2)}) async-start(f32[128,8,384]{2,1,0:T(8,128)} %bitcast.12), calls=%async_computation.2 | async-start | bytes 3145728 | tf_op jit(solution)/shard_map/all_to_all | solution.py:12
  191.0 0.1 copy.30
  191.1 0.1 reshape.89
  191.2 24.7 %all-to-all-done.2 = f32[128,8,384]{2,1,0:T(8,128)S(1)} async-done(((f32[128,8,384]{2,1,0:T(8,128)}), f32[128,8,384]{2,1,0:T(8,128)S(1)}, u32[]{:S(2)}, u32[]{:S(2)}) %all-to-all-start.2) | async-done | bytes 1572896 | tf_op jit(solution)/shard_map/all_to_all | solution.py:12
  215.9 7.1 %scatter_custom_fusion.1 = f32[1024,384]{1,0:T(8,128)S(1)} fusion(s32[1024]{0:T(1024)S(1)} %reshape.89, f32[128,8,384]{2,1,0:T(8,128)S(1)} %all-to-all-done.2, f32[]{:T(128)} %constant.4.clone.1), kind=kCustom, calls=%fused_computation.11 | custom fusion | flops 393216 | bytes 3145732 | tf_op jit(solution)/shard_map/scatter-add | solution.py:69
  223.0 0.5 copy.37
  223.5 1.1 copy.38
  224.5 0.0 copy-start.1
  224.6 28.6 %all_to_all.43 = f32[3,128,1024]{2,0,1:T(4,128)S(1)} all-to-all(f32[3,128,1024]{2,0,1:T(4,128)S(1)} %copy.38), channel_id=1, replica_groups=mesh['lev'=4,'col'=32] {'lev'}, dimensions={1} | all-to-all | bytes 3145728 | tf_op jit(solution)/shard_map/all_to_all | solution.py:75
  253.2 0.9 copy.39
  254.1 1.3 copy.44
  255.4 0.0 copy-done.1
  (13 shorter events, 0.0 us)
Async XLA Ops:
  0.0 52.6 %copy-start = (f32[8,8192]{1,0:T(8,128)S(1)}, f32[8,8192]{1,0:T(8,128)}, u32[]{:S(2)}) copy-start(f32[8,8192]{1,0:T(8,128)} %param.12) | copy-start | bytes 786436
  6.0 10.1 %copy-start.5 = (s32[1,128,8]{1,2,0:T(8,128)S(1)}, s32[1,128,8]{1,2,0:T(8,128)}, u32[]{:S(2)}) copy-start(s32[1,128,8]{1,2,0:T(8,128)} %param.16) | copy-start | bytes 12292
  6.0 10.4 %copy-start.6 = (f32[616]{0:T(1024)S(1)}, f32[616]{0:T(1024)}, u32[]{:S(2)}) copy-start(f32[616]{0:T(1024)} %param.14) | copy-start | bytes 7396
  6.0 10.4 %copy-start.4 = (s32[8,616]{1,0:T(8,128)S(1)}, s32[8,616]{1,0:T(8,128)}, u32[]{:S(2)}) copy-start(s32[8,616]{1,0:T(8,128)} %param.15) | copy-start | bytes 59140
  6.0 10.4 %copy-start.2 = (s32[8192]{0:T(1024)S(1)}, s32[8192]{0:T(1024)}, u32[]{:S(2)}) copy-start(s32[8192]{0:T(1024)} %param.17) | copy-start | bytes 98308
  11.6 16.8 %all-to-all-start = ((bf16[4,2,49152]{2,1,0:T(2,128)(2,1)}), bf16[4,2,49152]{2,1,0:T(2,128)(2,1)S(1)}, u32[]{:S(2)}, u32[]{:S(2)}) async-start(bf16[4,2,49152]{2,1,0:T(2,128)(2,1)} %reshape.103), calls=%async_computation | async-start | bytes 1572864 | tf_op jit(solution)/shard_map/all_to_all | solution.py:57
  38.3 14.2 %copy-start.3 = (f32[616,8]{0,1:T(8,128)S(1)}, f32[616,8]{0,1:T(8,128)}, u32[]{:S(2)}) copy-start(f32[616,8]{0,1:T(8,128)} %param.13) | copy-start | bytes 59140
  43.4 30.0 %all-to-all-start.1 = ((bf16[128,8,384]{2,1,0:T(8,128)(2,1)}), bf16[128,8,384]{2,1,0:T(8,128)(2,1)S(1)}, u32[]{:S(2)}, u32[]{:S(2)}) async-start(bf16[128,8,384]{2,1,0:T(8,128)(2,1)} %bitcast.7), calls=%async_computation.1 | async-start | bytes 1572864 | tf_op jit(solution)/shard_map/all_to_all | solution.py:8
  181.5 34.5 %all-to-all-start.2 = ((f32[128,8,384]{2,1,0:T(8,128)}), f32[128,8,384]{2,1,0:T(8,128)S(1)}, u32[]{:S(2)}, u32[]{:S(2)}) async-start(f32[128,8,384]{2,1,0:T(8,128)} %bitcast.12), calls=%async_computation.2 | async-start | bytes 3145728 | tf_op jit(solution)/shard_map/all_to_all | solution.py:12
  224.5 30.9 %copy-start.1 = (f32[8,8192]{1,0:T(8,128)S(1)}, f32[8,8192]{1,0:T(8,128)}, u32[]{:S(2)}) copy-start(f32[8,8192]{1,0:T(8,128)} %param.12) | copy-start | bytes 786436
where the time goes:
time: 256 us; the launch traced here: 255 us
  local copies, waits for them, and re-layouts  63.8 us (25%)
  other arithmetic  57.5 us (22%)
  matrix products  45.3 us (18%)
  waiting for transfers between devices  36.7 us (14%)
  blocking collectives  28.6 us (11%)
  starting transfers between devices  23.3 us (9%)
    scatter-add x1, other arithmetic, on_device(): jax.ops.segment_sum(adjoint, obs_slot, num_segments=peer_count * capacity)  50.4 us
    gather x1, local copies, waits for them, and re-layouts, on_device(): profile = incoming[obs_slot]  33.1 us
    all_to_all x1, blocking collectives, on_device(): lax.all_to_all(field_adjoint, 'lev', split_axis=1, concat_axis=2, tiled=T...  28.6 us
    all_to_all x1, waiting for transfers between devices, return_rows(): lax.all_to_all(outgoing, ('lev', 'col'), split_axis=0, concat_axis=0, til...  24.7 us
    dot_general x1, matrix products, observe(): jnp.einsum('tcf,cto->tof', jacobian, forcing, preferred_element_type=jnp....  24.5 us
    dot_general x1, matrix products, observe(): jnp.dot(bias_coef, predictor, precision=lax.Precision.HIGHEST, preferred_...  20.8 us
    unnamed x18, local copies, waits for them, and re-layouts  15.9 us
    all_to_all x1, waiting for transfers between devices, on_device(): lax.all_to_all(increment, 'lev', split_axis=2, concat_axis=1, tiled=True)  12 us
  transfers between devices with their start and end apart: 3, of which 2 were waited for; matrix products, arithmetic and copies ran while one was open for 8% of the time, Pallas kernels for 0%

commit v1 on v0

--- a/solution.py
+++ b/solution.py
@@ -2,6 +2,25 @@
 import jax.numpy as jnp
 from jax import lax
 from jax.sharding import PartitionSpec as P
+
+
+def review_series_all(vector, dimension_no, incoming_x):
+    reached = vector.shape
+    oldest = vector.reshape(
+        *reached[:dimension_no],
+        incoming_x,
+        reached[dimension_no] // incoming_x,
+        *reached[dimension_no + 1 :]
+    )
+    work_now = jnp.moveaxis(oldest, dimension_no, 0)
+    return work_now
+
+
+def numbers_link(t0, pos_dim):
+    last = list(t0.shape[1:])
+    last[pos_dim] *= t0.shape[0]
+    local_out = jnp.moveaxis(t0, 0, pos_dim).reshape(last)
+    return local_out
 
 
 def fetch_rows(outgoing):
@@ -54,7 +73,23 @@
     peer_count = lev_size * col_size
     field_count = increment.shape[0]
     capacity = send_cols.shape[2]
-    columns = lax.all_to_all(increment, "lev", split_axis=2, concat_axis=1, tiled=True)
+
+    def cover_kinds(frame_in, dev_axis, v0, local_array):
+        left_arr, before = (lax.axis_size(dev_axis), lax.axis_index(dev_axis))
+        upper = review_series_all(frame_in, v0, left_arr)
+        sheets = [upper[before]]
+        for t in [*range(1, left_arr)]:
+            t1 = upper[before ^ t]
+            sheets.append(
+                lax.ppermute(
+                    t1, axis_name=dev_axis, perm=[(idx, idx ^ t) for idx in range(left_arr)]
+                )
+            )
+        upper = jnp.stack(sheets)[before ^ jnp.arange(left_arr)]
+        m_next = numbers_link(upper, local_array)
+        return m_next
+
+    columns = cover_kinds(increment, "lev", 2, 1)
     level_count = columns.shape[1]
     column_count = columns.shape[2]
     profile_len = field_count * level_count

time: 256 us -> 239 us (0.934)
  local copies, waits for them, and re-layouts: 63.8 us -> 47.8 us
    unnamed x18 -> x19, local copies, waits for them, and re-layouts: 15.9 us -> 0.39 us
    all_to_all x1 -> x0, waiting for transfers between devices: 12 us -> none  [on_device(): lax.all_to_all(increment, 'lev', split_axis=2, concat_axis=1, tiled=True)]
    ppermute x0 -> x3, waiting for transfers between devices: none -> 11 us  [cover_kinds(): lax.ppermute(t1, axis_name=dev_axis, perm=[(idx, idx ^ t) for idx in rang...]
    all_to_all x1 -> x0, local copies, waits for them, and re-layouts: 5.34 us -> none  [on_device(): lax.all_to_all(increment, 'lev', split_axis=2, concat_axis=1, tiled=True)]
    ppermute x0 -> x3, starting transfers between devices: none -> 4.94 us  [cover_kinds(): lax.ppermute(t1, axis_name=dev_axis, perm=[(idx, idx ^ t) for idx in rang...]
    all_to_all x1 -> x0, starting transfers between devices: 4.55 us -> none  [on_device(): lax.all_to_all(increment, 'lev', split_axis=2, concat_axis=1, tiled=True)]
  transfers between devices with their start and end apart: 3 -> 5, of which waited for: 2 -> 4; matrix products, arithmetic and copies ran while one was open for 8% -> 9% of each run, Pallas kernels for 0% -> 0%
where the time goes in v1:
time: 239 us; the launch traced here: 238 us
  other arithmetic  57.7 us (24%)
  local copies, waits for them, and re-layouts  47.8 us (20%)
  matrix products  45.3 us (19%)
  waiting for transfers between devices  35.6 us (15%)
  blocking collectives  28.6 us (12%)
  starting transfers between devices  23.1 us (10%)
    scatter-add x1, other arithmetic, on_device(): jax.ops.segment_sum(adjoint, obs_slot, num_segments=peer_count * capacity)  50.4 us
    gather x1, local copies, waits for them, and re-layouts, on_device(): profile = incoming[obs_slot]  33.1 us
    all_to_all x1, blocking collectives, on_device(): lax.all_to_all(field_adjoint, 'lev', split_axis=1, concat_axis=2, tiled=T...  28.6 us
    all_to_all x1, waiting for transfers between devices, return_rows(): lax.all_to_all(outgoing, ('lev', 'col'), split_axis=0, concat_axis=0, til...  24.7 us
    dot_general x1, matrix products, observe(): jnp.einsum('tcf,cto->tof', jacobian, forcing, preferred_element_type=jnp....  24.5 us
    dot_general x1, matrix products, observe(): jnp.dot(bias_coef, predictor, precision=lax.Precision.HIGHEST, preferred_...  20.8 us
    ppermute x3, waiting for transfers between devices, cover_kinds(): lax.ppermute(t1, axis_name=dev_axis, perm=[(idx, idx ^ t) for idx in rang...  11 us
    all_to_all x1, starting transfers between devices, return_rows(): lax.all_to_all(outgoing, ('lev', 'col'), split_axis=0, concat_axis=0, til...  9.6 us
  transfers between devices with their start and end apart: 5, of which 4 were waited for; matrix products, arithmetic and copies ran while one was open for 9% of the time, Pallas kernels for 0%

profile of v1, /device:TPU:0, one launch (start us, length us, event | category | flops | bytes accessed | tf_op | source)
XLA Modules:
  0.0 238.4 jit_solution(13486764975508423433)
XLA Ops:
  0.0 2.4 reshape.77
  2.4 1.8 constant_dynamic-slice_fusion.3
  4.2 0.1 copy.53
  4.3 1.7 collective-permute-start
  6.1 0.1 copy.52
  6.1 3.0 %collective-permute-start.1 = (bf16[3,32,1024]{2,1,0:T(8,128)(2,1)S(1)}, bf16[3,32,1024]{2,1,0:T(8,128)(2,1)S(1)}, u32[]{:S(2)}, u32[]{:S(2)}) collective-permute-start(bf16[3,32,1024]{2,1,0:T(8,128)(2,1)S(1)} %bitcast.71), channel_id=1, source_target_pairs={{0,64},{32,96},{64,0},{96,32},{1,65},{33,97},{65,1},{97,33},{2,66}... | collective-permute-start | bytes 589832 | tf_op jit(solution)/shard_map/ppermute | solution.py:84
  9.1 0.1 copy.51
  9.2 0.2 collective-permute-start.2
  9.5 0.1 copy.33
  9.6 0.1 reshape.95
  9.8 2.4 %collective-permute-done = bf16[3,32,1024]{2,1,0:T(8,128)(2,1)S(1)} collective-permute-done((bf16[3,32,1024]{2,1,0:T(8,128)(2,1)S(1)}, bf16[3,32,1024]{2,1,0:T(8,128)(2,1)S(1)}, u32[]{:S(2)}, u32[]{:S(2)}) %collective-permute-start) | collective-permute-done | bytes 196640 | tf_op jit(solution)/shard_map/ppermute | solution.py:84
  12.2 5.7 %collective-permute-done.1 = bf16[3,32,1024]{2,1,0:T(8,128)(2,1)S(1)} collective-permute-done((bf16[3,32,1024]{2,1,0:T(8,128)(2,1)S(1)}, bf16[3,32,1024]{2,1,0:T(8,128)(2,1)S(1)}, u32[]{:S(2)}, u32[]{:S(2)}) %collective-permute-start.1) | collective-permute-done | bytes 196640 | tf_op jit(solution)/shard_map/ppermute | solution.py:84
  17.9 2.9 %collective-permute-done.2 = bf16[3,32,1024]{2,1,0:T(8,128)(2,1)S(1)} collective-permute-done((bf16[3,32,1024]{2,1,0:T(8,128)(2,1)S(1)}, bf16[3,32,1024]{2,1,0:T(8,128)(2,1)S(1)}, u32[]{:S(2)}, u32[]{:S(2)}) %collective-permute-start.2) | collective-permute-done | bytes 196640 | tf_op jit(solution)/shard_map/ppermute | solution.py:84
  20.8 0.1 pad_maximum_fusion
  20.9 0.6 gather_fusion
  21.5 0.4 copy.32
  21.9 5.0 %gather_fusion.1 = bf16[1024,384]{1,0:T(8,128)(2,1)} fusion(bf16[1024,384]{1,0:T(8,128)(2,1)S(1)} %bitcast.58, s32[1024]{0:T(1024)S(1)} %broadcast_clamp_fusion), kind=kCustom, calls=%fused_computation.1 | custom fusion | bytes 1576960 | tf_op jit(solution)/shard_map/gather | solution.py:98
  26.9 8.6 %all-to-all-start = ((bf16[128,8,384]{2,1,0:T(8,128)(2,1)}), bf16[128,8,384]{2,1,0:T(8,128)(2,1)S(1)}, u32[]{:S(2)}, u32[]{:S(2)}) async-start(bf16[128,8,384]{2,1,0:T(8,128)(2,1)} %bitcast.9), calls=%async_computation | async-start | bytes 1572864 | tf_op jit(solution)/shard_map/all_to_all | solution.py:27
  35.5 20.8 %convert_subtract_fusion = f32[616,8192]{1,0:T(8,128)} fusion(bf16[616,8192]{1,0:T(8,128)(2,1)} %param.11, f32[616,8]{0,1:T(8,128)S(1)} %copy-done.3, f32[8,8192]{1,0:T(8,128)S(1)} %copy-done), kind=kOutput, calls=%fused_computation.8 | convolution fusion | flops 494534656 | bytes 30559488 | tf_op jit(solution)/shard_map/dot_general | solution.py:46
  56.3 33.1 %gather_fusion.2 = bf16[8192,384]{1,0:T(8,128)(2,1)} fusion(bf16[1024,384]{1,0:T(8,128)(2,1)S(1)} %bitcast.57, s32[8192]{0:T(1024)S(1)} %fusion.12), kind=kCustom, calls=%fused_computation.2 | custom fusion | bytes 12615680 | tf_op jit(solution)/shard_map/gather | solution.py:100
  89.4 24.5 %fusion.2 = f32[8,1024,384]{2,1,0:T(8,128)} fusion(bf16[8,616,384]{2,1,0:T(8,128)(2,1)} %param.10, f32[77,8,8,1024]{3,2,1,0:T(8,128)} %bitcast.59, f32[616,8]{0,1:T(8,128)S(1)} %multiply_bitcast_fusion, bf16[8,1024,384]{2,1,0:T(8,128)(2,1)} %bitcast.60), kind=kOutput, calls=%fused_computation.9 | convolution fusion | flops 7766212608 | bytes 42863872 | tf_op jit(solution)/shard_map/tcf,cto->tof/dot_general | solution.py:55
  113.9 50.4 %scatter_custom_fusion = f32[1024,384]{1,0:T(8,128)} fusion(s32[8192]{0:T(1024)S(1)} %copy-done.2, f32[8192,384]{1,0:T(8,128)} %bitcast.73, f32[]{:T(128)} %constant.10.clone.1), kind=kCustom, calls=%fused_computation.16 | custom fusion | flops 3145728 | bytes 1573376 | tf_op jit(solution)/shard_map/scatter-add | solution.py:102
  164.4 9.6 %all-to-all-start.1 = ((f32[128,8,384]{2,1,0:T(8,128)}), f32[128,8,384]{2,1,0:T(8,128)S(1)}, u32[]{:S(2)}, u32[]{:S(2)}) async-start(f32[128,8,384]{2,1,0:T(8,128)} %bitcast.14), calls=%async_computation.1 | async-start | bytes 3145728 | tf_op jit(solution)/shard_map/all_to_all | solution.py:31
  174.0 0.1 copy.30
  174.1 0.1 reshape.119
  174.2 24.7 %all-to-all-done.1 = f32[128,8,384]{2,1,0:T(8,128)S(1)} async-done(((f32[128,8,384]{2,1,0:T(8,128)}), f32[128,8,384]{2,1,0:T(8,128)S(1)}, u32[]{:S(2)}, u32[]{:S(2)}) %all-to-all-start.1) | async-done | bytes 1572896 | tf_op jit(solution)/shard_map/all_to_all | solution.py:31
  198.8 7.1 %scatter_custom_fusion.1 = f32[1024,384]{1,0:T(8,128)S(1)} fusion(s32[1024]{0:T(1024)S(1)} %reshape.119, f32[128,8,384]{2,1,0:T(8,128)S(1)} %all-to-all-done.1, f32[]{:T(128)} %constant.10.clone.1), kind=kCustom, calls=%fused_computation.12 | custom fusion | flops 393216 | bytes 3145732 | tf_op jit(solution)/shard_map/scatter-add | solution.py:104
  205.9 0.5 copy.35
  206.4 1.1 copy.36
  207.5 28.6 %all_to_all.28 = f32[3,128,1024]{2,0,1:T(4,128)S(1)} all-to-all(f32[3,128,1024]{2,0,1:T(4,128)S(1)} %copy.36), channel_id=1, replica_groups=mesh['lev'=4,'col'=32] {'lev'}, dimensions={1} | all-to-all | bytes 3145728 | tf_op jit(solution)/shard_map/all_to_all | solution.py:110
  236.1 0.9 copy.37
  237.0 1.3 copy.44
  (24 shorter events, 0.2 us)
Async XLA Ops:
  0.0 35.5 %copy-start = (f32[8,8192]{1,0:T(8,128)S(1)}, f32[8,8192]{1,0:T(8,128)}, u32[]{:S(2)}) copy-start(f32[8,8192]{1,0:T(8,128)} %param.12) | copy-start | bytes 786436
  0.0 9.5 %copy-start.5 = (s32[1,128,8]{1,2,0:T(8,128)S(1)}, s32[1,128,8]{1,2,0:T(8,128)}, u32[]{:S(2)}) copy-start(s32[1,128,8]{1,2,0:T(8,128)} %param.16) | copy-start | bytes 12292
  0.0 9.7 %copy-start.2 = (s32[8192]{0:T(1024)S(1)}, s32[8192]{0:T(1024)}, u32[]{:S(2)}) copy-start(s32[8192]{0:T(1024)} %param.17) | copy-start | bytes 98308
  0.0 9.7 %copy-start.6 = (f32[616]{0:T(1024)S(1)}, f32[616]{0:T(1024)}, u32[]{:S(2)}) copy-start(f32[616]{0:T(1024)} %param.14) | copy-start | bytes 7396
  0.0 9.7 %copy-start.4 = (s32[8,616]{1,0:T(8,128)S(1)}, s32[8,616]{1,0:T(8,128)}, u32[]{:S(2)}) copy-start(s32[8,616]{1,0:T(8,128)} %param.15) | copy-start | bytes 59140
  4.3 7.9 %collective-permute-start = (bf16[3,32,1024]{2,1,0:T(8,128)(2,1)S(1)}, bf16[3,32,1024]{2,1,0:T(8,128)(2,1)S(1)}, u32[]{:S(2)}, u32[]{:S(2)}) collective-permute-start(bf16[3,32,1024]{2,1,0:T(8,128)(2,1)S(1)} %bitcast.70), channel_id=1, source_target_pairs={{0,32},{32,0},{64,96},{96,64},{1,33},{33,1},{65,97},{97,65},{2,34}... | collective-permute-start | bytes 589832 | tf_op jit(solution)/shard_map/ppermute | solution.py:84
  6.1 11.8 %collective-permute-start.1 = (bf16[3,32,1024]{2,1,0:T(8,128)(2,1)S(1)}, bf16[3,32,1024]{2,1,0:T(8,128)(2,1)S(1)}, u32[]{:S(2)}, u32[]{:S(2)}) collective-permute-start(bf16[3,32,1024]{2,1,0:T(8,128)(2,1)S(1)} %bitcast.71), channel_id=1, source_target_pairs={{0,64},{32,96},{64,0},{96,32},{1,65},{33,97},{65,1},{97,33},{2,66}... | collective-permute-start | bytes 589832 | tf_op jit(solution)/shard_map/ppermute | solution.py:84
  9.2 11.6 %collective-permute-start.2 = (bf16[3,32,1024]{2,1,0:T(8,128)(2,1)S(1)}, bf16[3,32,1024]{2,1,0:T(8,128)(2,1)S(1)}, u32[]{:S(2)}, u32[]{:S(2)}) collective-permute-start(bf16[3,32,1024]{2,1,0:T(8,128)(2,1)S(1)} %bitcast.72), channel_id=1, source_target_pairs={{0,96},{32,64},{64,32},{96,0},{1,97},{33,65},{65,33},{97,1},{2,98}... | collective-permute-start | bytes 589832 | tf_op jit(solution)/shard_map/ppermute | solution.py:84
  21.9 13.6 %copy-start.3 = (f32[616,8]{0,1:T(8,128)S(1)}, f32[616,8]{0,1:T(8,128)}, u32[]{:S(2)}) copy-start(f32[616,8]{0,1:T(8,128)} %param.13) | copy-start | bytes 59140
  26.9 29.4 %all-to-all-start = ((bf16[128,8,384]{2,1,0:T(8,128)(2,1)}), bf16[128,8,384]{2,1,0:T(8,128)(2,1)S(1)}, u32[]{:S(2)}, u32[]{:S(2)}) async-start(bf16[128,8,384]{2,1,0:T(8,128)(2,1)} %bitcast.9), calls=%async_computation | async-start | bytes 1572864 | tf_op jit(solution)/shard_map/all_to_all | solution.py:27
  164.4 34.5 %all-to-all-start.1 = ((f32[128,8,384]{2,1,0:T(8,128)}), f32[128,8,384]{2,1,0:T(8,128)S(1)}, u32[]{:S(2)}, u32[]{:S(2)}) async-start(f32[128,8,384]{2,1,0:T(8,128)} %bitcast.14), calls=%async_computation.1 | async-start | bytes 3145728 | tf_op jit(solution)/shard_map/all_to_all | solution.py:31
  207.5 30.9 %copy-start.1 = (f32[8,8192]{1,0:T(8,128)S(1)}, f32[8,8192]{1,0:T(8,128)}, u32[]{:S(2)}) copy-start(f32[8,8192]{1,0:T(8,128)} %param.12) | copy-start | bytes 786436
